TPU v7x, 32 devices: a whole 2x2x4 slice. The times are simulated.
32 devices in a mesh: seq: 8 (over y, x, core), rep: 4 (over z).
Axes of the slice: x: 2, y: 2, z: 4, core: 2. Of those that a mesh axis runs over, the one named last changes fastest.
Arguments:
- tokens: bfloat16 [4, 1024, 1024], P('rep', 'seq'), may hold values from -16 to 16
- cotangent: bfloat16 [4, 1024, 1024], P('rep', 'seq'), may hold values from -6 to 6
- weights: bfloat16 [4, 1024, 512], replicated, may hold values from -0.1875 to 0.1875
- neighbour_lists: int32 [4, 8, 27], P('rep'), may hold values from 0 to 7, as said below
- neighbour_counts: int32 [4, 8], P('rep'), may hold values from 1 to 8, as said below
Outputs:
- output: bfloat16 [4, 1024, 1024], P('rep', 'seq')
- d_inputs: bfloat16 [4, 1024, 1024], P('rep', 'seq')
- weight_grads: float32 [4, 1024, 512], P(None, ('seq', 'rep'))
Inputs may be any that keep to these rules, and one draw needn't show every extreme that they name: `neighbour_lists`: slot 0 of every list is the block itself; the live slots of a list name distinct blocks of the same replica's slab; dead slots hold the block's own position. `neighbour_counts`: in each replica some block has min(27, 8) live slots.
All inputs are finite; a program needn't handle non-finite values.
Results may differ from a plain program's by a relative error of at most 0.023.
The roundings to bfloat16 on the way count: a program that leaves them out, or rounds other values in their place, can miss the bound.
Values may be sent and summed in bfloat16 or wider, within the bound.
A program may use at most 128 MiB of HBM per device.

v0:
```python
import functools
import math

import jax
import jax.numpy as jnp
from jax import lax
from jax.experimental import pallas as pl
from jax.experimental.pallas import tpu as pltpu
from jax.sharding import PartitionSpec as P

HEADS = 8
HEAD_DIM = 64
BLOCK = 128
MAXN = 27


F32 = jnp.float32
BF16 = jnp.bfloat16


def mm(a, b):
    return jnp.dot(a, b, preferred_element_type=F32)


def mm_nt(a, b):
    return lax.dot_general(a, b, (((1,), (1,)), ((), ())), preferred_element_type=F32)


def layer_kernel(
    n, reps,
    tok_hbm, cot_hbm, w_hbm, lists, counts,
    out, dinp, grads,
    tok, cot, w, send1, recv1, tstage, trecv, kt, vt, qtr, dtr, kx, vx, dkt, dvt, bias,
    normed_all, e_all, total_all, att_all, dq_all, xp, bk, back, gs, gr,
    ls, ss1, rs1, sst, rst, srl, ssb, rsb, ssp, rsp, ssg, rsg,
):
    me = lax.axis_index("seq")
    rep = lax.axis_index("rep")
    core = lax.rem(me, 2)
    chip = me // 2
    chips = n // 2
    scale = 1.0 / math.sqrt(HEAD_DIM)
    hd = HEAD_DIM
    part = gs.shape[2]

    loads = [
        pltpu.make_async_copy(tok_hbm.at[0], tok, ls.at[0]),
        pltpu.make_async_copy(cot_hbm.at[0], cot, ls.at[1]),
    ] + [pltpu.make_async_copy(w_hbm.at[j], w.at[j], ls.at[2 + j]) for j in range(4)]
    for load in loads:
        load.start()

    def remote(src, dst, s_sem, r_sem, seq, z):
        return pltpu.make_async_remote_copy(
            src_ref=src, dst_ref=dst, send_sem=s_sem, recv_sem=r_sem,
            device_id={"seq": seq, "rep": z}, device_id_type=pl.DeviceIdType.MESH,
        )

    barrier = pltpu.get_barrier_semaphore()

    def greet_seq(i, carry):
        pl.semaphore_signal(
            barrier, inc=1, device_id={"seq": lax.rem(me + i, n), "rep": rep},
            device_id_type=pl.DeviceIdType.MESH,
        )
        return carry

    def greet_rep(i, carry):
        pl.semaphore_signal(
            barrier, inc=1,
            device_id={
                "seq": lax.rem(me + 2 * lax.rem(i, chips), n),
                "rep": lax.rem(rep + 1 + i // chips, reps),
            },
            device_id_type=pl.DeviceIdType.MESH,
        )
        return carry

    lax.fori_loop(1, n, greet_seq, 0)
    lax.fori_loop(0, (reps - 1) * chips, greet_rep, 0)

    def each_peer(act):
        def step(i, carry):
            act(lax.rem(me + i, n))
            return carry

        lax.fori_loop(1, n, step, 0)

    x_chip = chip + 1 - 2 * lax.rem(chip, 2)
    y_chip = chip + 2 - 4 * (chip // 2)
    far_chip = chips - 1 - chip
    other = me + 1 - 2 * core

    def stage_cols(kind, ref):
        for s in range(n):
            cols = slice((s // 2) * BLOCK, (s // 2 + 1) * BLOCK)
            tstage[s % 2, kind, :, cols] = ref[:, s * BLOCK : (s + 1) * BLOCK]

    def cols_out(to, kind):
        return remote(
            tstage.at[lax.rem(to, 2), kind], trecv.at[me, kind],
            sst.at[kind, to], rst.at[kind, me], to, rep,
        )

    def cols_in(src, kind):
        return remote(
            tstage.at[core, kind], trecv.at[src, kind],
            sst.at[kind, src], rst.at[kind, src], src, rep,
        )

    def cols_on(kind, k):
        src, to = (y_chip, x_chip) if kind == 0 else (x_chip, y_chip)
        block = 2 * src + k
        return remote(
            trecv.at[block, kind], trecv.at[block, kind],
            srl.at[kind, k], rst.at[kind, block], 2 * to + core, rep,
        )

    def near(kind, act):
        act(other, kind)
        for k in range(2):
            act(2 * x_chip + k, kind)
            act(2 * y_chip + k, kind)

    def forward_cols(kind):
        for k in range(2):
            cols_in(2 * (y_chip if kind == 0 else x_chip) + k, kind).wait_recv()
            cols_on(kind, k).start()

    def finish_cols(kind):
        cols_in(other, kind).wait_recv()
        for k in range(2):
            cols_in(2 * (x_chip if kind == 0 else y_chip) + k, kind).wait_recv()
            cols_in(2 * far_chip + k, kind).wait_recv()

    loads[0].wait()
    stage_cols(0, tok)
    pl.semaphore_wait(barrier, n - 1 + (reps - 1) * chips)
    near(0, lambda to, kind: cols_out(to, kind).start())
    loads[1].wait()
    stage_cols(1, cot)

    def heads_out(to, piece):
        return remote(
            send1.at[to, piece], recv1.at[me, piece],
            ss1.at[piece, to], rs1.at[piece, me], to, rep,
        )

    def heads_in(src, piece):
        return remote(
            send1.at[src, piece], recv1.at[src, piece],
            ss1.at[piece, src], rs1.at[piece, src], src, rep,
        )

    def pack(piece, one, two):
        for h in range(n):
            cols = slice(h * hd, (h + 1) * hd)
            send1[h, piece] = jnp.concatenate([one[:, cols], two[:, cols]], axis=1)
        each_peer(lambda to: heads_out(to, piece).start())
        recv1[me, piece] = send1[me, piece]

    x = tok[...]
    loads[2].wait()
    q = (mm(x, w[0]).astype(BF16).astype(F32) * scale).astype(BF16)
    loads[3].wait()
    k = mm(x, w[1]).astype(BF16)
    pack(0, q, k)
    loads[4].wait()
    v = mm(x, w[2]).astype(BF16)
    loads[5].wait()
    da = mm(cot[...], w[3]).astype(BF16)
    pack(1, v, da)
    near(1, lambda to, kind: cols_out(to, kind).start())

    trecv[pl.ds(me, 1)] = tstage[pl.ds(core, 1)]

    eye = lax.broadcasted_iota(jnp.int32, (n, n), 0) == lax.broadcasted_iota(jnp.int32, (n, n), 1)
    count_col = jnp.sum(
        jnp.where(eye, jnp.broadcast_to(counts[...].astype(F32), (n, n)), 0.0),
        axis=1, keepdims=True,
    )
    listed = lists[0]
    slot = lax.broadcasted_iota(jnp.int32, listed.shape, 1).astype(F32)
    alive = slot < count_col
    for c in range(n):
        hit = jnp.max(
            jnp.where(jnp.logical_and(listed == c, alive), 1.0, 0.0), axis=1, keepdims=True
        )
        bias[:, c * BLOCK : (c + 1) * BLOCK] = jnp.broadcast_to((hit - 1.0) * 1e30, (n, BLOCK))
    dkt[...] = jnp.zeros_like(dkt)
    dvt[...] = jnp.zeros_like(dvt)

    each_peer(lambda src: heads_in(src, 0).wait_recv())
    for b in range(n):
        rows = slice(b * BLOCK, (b + 1) * BLOCK)
        qk = recv1[b, 0]
        kx[rows] = qk[:, hd:]
        qkt = qk.T
        qtr[:, rows] = qkt[:hd]
        kt[:, rows] = qkt[hd:]

    def back_out(b, piece):
        rows = pl.ds(pl.multiple_of(b * BLOCK, BLOCK), BLOCK)
        return remote(
            bk.at[piece, rows], back.at[me, piece],
            ssb.at[piece, b], rsb.at[piece, me], b, rep,
        )

    def back_in(h, piece):
        return remote(
            bk.at[piece, pl.ds(0, BLOCK)], back.at[h, piece],
            ssb.at[piece, h], rsb.at[piece, h], h, rep,
        )

    def pair_out(piece):
        return remote(
            xp.at[core, piece], xp.at[core, piece], ssp.at[piece], rsp.at[piece], other, rep
        )

    def pair_in(piece):
        return remote(
            xp.at[1 - core, piece], xp.at[1 - core, piece],
            ssp.at[piece], rsp.at[piece], other, rep,
        )

    def pair_of(i):
        return pl.ds(pl.multiple_of(2 * i * BLOCK, 2 * BLOCK), 2 * BLOCK)

    def two_blocks(i, piece):
        return recv1[pl.ds(2 * i, 2), piece].reshape(2 * BLOCK, 2 * hd)

    def weigh(i, carry):
        rows = pair_of(i)
        mask = [
            jnp.broadcast_to(bias[pl.ds(2 * i + j, 1), :], (BLOCK, n * BLOCK)) for j in range(2)
        ]
        s = mm(two_blocks(i, 0)[:, :hd], kt[...]) + jnp.concatenate(mask, axis=0)
        e = jnp.exp(s - jnp.max(s, axis=1, keepdims=True))
        total = jnp.sum(e, axis=1, keepdims=True)
        e_all[rows] = e.astype(BF16)
        total_all[rows] = total
        normed_all[rows] = e * (1.0 / total)
        return carry

    def forward(i, carry):
        rows = pair_of(i)
        att = (mm(e_all[rows], vx[...]) / total_all[rows]).astype(BF16)
        att_all[rows] = att
        xp[core, 0, :hd, rows] = att.T
        dvt[...] += mm(dtr[:, rows], normed_all[rows].astype(BF16))
        return carry

    forward_cols(0)
    lax.fori_loop(0, n // 2, weigh, 0, unroll=2)
    each_peer(lambda src: heads_in(src, 1).wait_recv())
    for b in range(n):
        rows = slice(b * BLOCK, (b + 1) * BLOCK)
        vd = recv1[b, 1]
        vx[rows] = vd[:, :hd]
        vdt = vd.T
        vt[:, rows] = vdt[:hd]
        dtr[:, rows] = vdt[hd:]

    lax.fori_loop(0, n // 2, forward, 0, unroll=2)
    xp[core, 0, hd:] = dvt[...].astype(BF16)
    pair_out(0).start()

    for b in range(n):
        rows = slice(b * BLOCK, (b + 1) * BLOCK)
        bk[0, rows] = jnp.concatenate([att_all[rows], dvt[:, rows].T.astype(BF16)], axis=1)
    each_peer(lambda to: back_out(to, 0).start())

    def backward(i, carry):
        rows = pair_of(i)
        dab = two_blocks(i, 1)[:, hd:]
        delta = jnp.sum(dab.astype(F32) * att_all[rows].astype(F32), axis=1, keepdims=True)
        ds = (normed_all[rows] * (mm(dab, vt[...]) - delta)).astype(BF16)
        dkt[...] += mm(qtr[:, rows], ds)
        dq = (mm(ds, kx[...]) * scale).astype(BF16)
        dq_all[rows] = dq
        xp[core, 1, :hd, rows] = dq.T
        return carry

    def grads_out(i, k0, count, stage):
        chip_to = lax.rem(chip + i, chips)
        rep_to = lax.rem(rep + i // chips, reps)
        to = chip_to * reps + rep_to
        here = chip * reps + rep
        return remote(
            gs.at[to, pl.ds(k0, count)], gr.at[here, pl.ds(k0, count)],
            ssg.at[stage, to], rsg.at[stage, here], 2 * chip_to + core, rep_to,
        )

    def grads_in(i, k0, count, stage):
        chip_from = lax.rem(chip + i, chips)
        rep_from = lax.rem(rep + i // chips, reps)
        src = chip_from * reps + rep_from
        return remote(
            gs.at[src, pl.ds(k0, count)], gr.at[src, pl.ds(k0, count)],
            ssg.at[stage, src], rsg.at[stage, src], 2 * chip_from + core, rep_from,
        )

    stages = ((2, 1, 0), (3, 1, 1), (0, 2, 2))

    def each_group(act):
        def step(i, carry):
            act(i)
            return carry

        lax.fori_loop(1, chips * reps, step, 0)

    def product(kinds, column_kind, piece, rows):
        left = jnp.concatenate(
            [xp[c, piece][r] for r in rows for c in range(2)], axis=0
        )
        right = trecv[:, column_kind].reshape(n * BLOCK, trecv.shape[3])
        total = mm(left, right).astype(BF16)
        for j, kind in enumerate(kinds):
            one = total[2 * hd * j : 2 * hd * (j + 1)].T
            gs[:, kind] = one.reshape(chips * reps, part, 2 * hd)

    low, high = slice(0, hd), slice(hd, 2 * hd)
    lax.fori_loop(0, 2, backward, 0, unroll=2)
    forward_cols(1)
    finish_cols(0)
    pair_in(0).wait_recv()
    product((2,), 0, 0, (high,))
    each_group(lambda i: grads_out(i, *stages[0]).start())
    lax.fori_loop(2, n // 2, backward, 0, unroll=2)

    xp[core, 1, hd:] = dkt[...].astype(BF16)
    pair_out(1).start()
    finish_cols(1)
    product((3,), 1, 0, (low,))
    each_group(lambda i: grads_out(i, *stages[1]).start())
    pair_in(1).wait_recv()
    product((0, 1), 0, 1, (low, high))
    each_group(lambda i: grads_out(i, *stages[2]).start())
    gr[pl.ds(chip * reps + rep, 1)] = gs[pl.ds(chip * reps + rep, 1)]

    for b in range(n):
        rows = slice(b * BLOCK, (b + 1) * BLOCK)
        bk[1, rows] = jnp.concatenate([dq_all[rows], dkt[:, rows].T.astype(BF16)], axis=1)
    each_peer(lambda to: back_out(to, 1).start())
    mine = pl.ds(pl.multiple_of(me * BLOCK, BLOCK), BLOCK)
    for piece in range(2):
        back[me, piece] = bk[piece, mine]

    each_peer(lambda src: back_in(src, 0).wait_recv())
    att = jnp.concatenate([back[h, 0][:, :hd] for h in range(n)], axis=1)
    dv = jnp.concatenate([back[h, 0][:, hd:] for h in range(n)], axis=1)
    out[0] = mm_nt(att, w[3]).astype(BF16)
    each_peer(lambda src: back_in(src, 1).wait_recv())
    dq = jnp.concatenate([back[h, 1][:, :hd] for h in range(n)], axis=1)
    dk = jnp.concatenate([back[h, 1][:, hd:] for h in range(n)], axis=1)
    dinp[0] = (mm_nt(dq, w[0]) + mm_nt(dk, w[1]) + mm_nt(dv, w[2])).astype(BF16)

    def drain(to):
        for piece in range(2):
            heads_out(to, piece).wait_send()
            back_out(to, piece).wait_send()

    each_peer(drain)
    for kind in range(2):
        near(kind, lambda to, kind: cols_out(to, kind).wait_send())
        for k in range(2):
            cols_on(kind, k).wait_send()
    pair_out(0).wait_send()
    pair_out(1).wait_send()
    for stage in stages:
        each_group(lambda i, stage=stage: grads_out(i, *stage).wait_send())
        each_group(lambda i, stage=stage: grads_in(i, *stage).wait_recv())
        kinds = slice(stage[0], stage[0] + stage[1])
        for c in range(chips):
            acc = gr[c * reps, kinds].astype(F32)
            for r in range(1, reps):
                acc = acc + gr[c * reps + r, kinds].astype(F32)
            grads[kinds, :, c * 2 * hd : (c + 1) * 2 * hd] = acc


def by_heads(n, reps, tokens, cotangent, weights, neighbour_lists, neighbour_counts):
    width = tokens.shape[2]
    slab = n * BLOCK
    cols = weights.shape[2]
    part = width // (n * reps)
    groups = (n // 2) * reps
    vmem = pl.BlockSpec(memory_space=pltpu.VMEM)
    hbm = pl.BlockSpec(memory_space=pl.ANY)
    dma = pltpu.SemaphoreType.DMA
    return pl.pallas_call(
        functools.partial(layer_kernel, n, reps),
        out_shape=(
            jax.ShapeDtypeStruct(tokens.shape, BF16),
            jax.ShapeDtypeStruct(tokens.shape, BF16),
            jax.ShapeDtypeStruct((4, part, cols), F32),
        ),
        in_specs=[hbm] * 3 + [vmem] * 2,
        out_specs=(vmem, vmem, vmem),
        scratch_shapes=[
            pltpu.VMEM((BLOCK, width), BF16),
            pltpu.VMEM((BLOCK, width), BF16),
            pltpu.VMEM(weights.shape, BF16),
            pltpu.VMEM((n, 2, BLOCK, 2 * HEAD_DIM), BF16),
            pltpu.VMEM((n, 2, BLOCK, 2 * HEAD_DIM), BF16),
            pltpu.VMEM((2, 2, BLOCK, width // 2), BF16),
            pltpu.VMEM((n, 2, BLOCK, width // 2), BF16),
            pltpu.VMEM((HEAD_DIM, slab), BF16),
            pltpu.VMEM((HEAD_DIM, slab), BF16),
            pltpu.VMEM((HEAD_DIM, slab), BF16),
            pltpu.VMEM((HEAD_DIM, slab), BF16),
            pltpu.VMEM((slab, HEAD_DIM), BF16),
            pltpu.VMEM((slab, HEAD_DIM), BF16),
            pltpu.VMEM((HEAD_DIM, slab), F32),
            pltpu.VMEM((HEAD_DIM, slab), F32),
            pltpu.VMEM((n, slab), F32),
            pltpu.VMEM((slab, slab), F32),
            pltpu.VMEM((slab, slab), BF16),
            pltpu.VMEM((slab, 1), F32),
            pltpu.VMEM((slab, HEAD_DIM), BF16),
            pltpu.VMEM((slab, HEAD_DIM), BF16),
            pltpu.VMEM((2, 2, 2 * HEAD_DIM, slab), BF16),
            pltpu.VMEM((2, slab, 2 * HEAD_DIM), BF16),
            pltpu.VMEM((n, 2, BLOCK, 2 * HEAD_DIM), BF16),
            pltpu.VMEM((groups, 4, part, 2 * HEAD_DIM), BF16),
            pltpu.VMEM((groups, 4, part, 2 * HEAD_DIM), BF16),
            dma((6,)),
            dma((2, n)), dma((2, n)), dma((2, n)), dma((2, n)), dma((2, 2)),
            dma((2, n)), dma((2, n)),
            dma((2,)), dma((2,)), dma((3, groups)), dma((3, groups)),
        ],
        compiler_params=pltpu.CompilerParams(
            collective_id=0, has_side_effects=True, vmem_limit_bytes=53 * 1024 * 1024
        ),
        cost_estimate=pl.CostEstimate(
            flops=3 * 10**9, bytes_accessed=6 * 2**20, transcendentals=2**20
        ),
    )(tokens, cotangent, weights, neighbour_lists, neighbour_counts)


def split_heads(matrix):
    return matrix.reshape(matrix.shape[:-1] + (HEADS, HEAD_DIM))


def body(tokens, cotangent, weights, neighbour_lists, neighbour_counts):
    score_scale = 1.0 / math.sqrt(HEAD_DIM)
    inputs = tokens[0]
    upstream = cotangent[0]
    row_count = inputs.shape[0]
    local_blocks = row_count // BLOCK
    w_query, w_key, w_value, w_out = (weights[0], weights[1], weights[2], weights[3])
    queries = (
        jnp.dot(inputs, w_query, preferred_element_type=jnp.float32)
        .astype(jnp.bfloat16)
        .reshape(local_blocks, BLOCK, -1)
    )
    key_rows = (
        jnp.dot(inputs, w_key, preferred_element_type=jnp.float32)
        .astype(jnp.bfloat16)
        .reshape(local_blocks, BLOCK, -1)
    )
    value_rows = (
        jnp.dot(inputs, w_value, preferred_element_type=jnp.float32)
        .astype(jnp.bfloat16)
        .reshape(local_blocks, BLOCK, -1)
    )
    all_keys, all_values = (
        lax.all_gather(key_rows, "seq", axis=0, tiled=True),
        lax.all_gather(value_rows, "seq", axis=0, tiled=True),
    )
    slab_blocks = all_keys.shape[0]
    first_block = lax.axis_index("seq") * local_blocks
    lists_all = neighbour_lists[0]
    counts_all = neighbour_counts[0]
    my_lists = lax.dynamic_slice_in_dim(lists_all, first_block, local_blocks, 0)
    my_counts = lax.dynamic_slice_in_dim(counts_all, first_block, local_blocks, 0)
    slot_keys = split_heads(
        jnp.take(all_keys, my_lists, axis=0).reshape(local_blocks, MAXN * BLOCK, -1)
    )
    slot_values = split_heads(
        jnp.take(all_values, my_lists, axis=0).reshape(local_blocks, MAXN * BLOCK, -1)
    )
    query_heads = split_heads(queries)
    scores = (
        jnp.einsum("bqhd,bkhd->bhqk", query_heads, slot_keys, preferred_element_type=jnp.float32)
        * score_scale
    )
    live_cols = (jnp.arange(MAXN * BLOCK) // BLOCK)[None, :] < my_counts[:, None]
    scores = jnp.where(live_cols[:, None, None, :], scores, -1e30)
    row_max = jnp.max(scores, axis=-1)
    exponent = jnp.exp(scores - row_max[..., None])
    totals = jnp.sum(exponent, axis=-1)
    mixed = jnp.einsum(
        "bhqk,bkhd->bqhd",
        exponent.astype(jnp.bfloat16),
        slot_values,
        preferred_element_type=jnp.float32,
    )
    attended = (
        (mixed / jnp.transpose(totals, (0, 2, 1))[..., None])
        .astype(jnp.bfloat16)
        .reshape(row_count, -1)
    )
    output = lax.dot_general(
        attended, w_out, (((1,), (1,)), ((), ())), preferred_element_type=jnp.float32
    ).astype(jnp.bfloat16)
    d_attended = jnp.dot(upstream, w_out, preferred_element_type=jnp.float32).astype(jnp.bfloat16)
    grad_out = lax.dot_general(
        upstream, attended, (((0,), (0,)), ((), ())), preferred_element_type=jnp.float32
    )
    d_blocks = d_attended.reshape(local_blocks, BLOCK, -1)
    d_heads = split_heads(d_blocks)
    attended_heads = split_heads(attended.reshape(local_blocks, BLOCK, -1))
    row_delta = jnp.transpose(
        jnp.sum(d_heads.astype(jnp.float32) * attended_heads.astype(jnp.float32), axis=-1),
        (0, 2, 1),
    )
    normed = exponent / totals[..., None]
    d_probs = jnp.einsum(
        "bqhd,bkhd->bhqk", d_heads, slot_values, preferred_element_type=jnp.float32
    )
    d_scores = (normed * (d_probs - row_delta[..., None])).astype(jnp.bfloat16)
    d_queries = (
        (
            jnp.einsum("bhqk,bkhd->bqhd", d_scores, slot_keys, preferred_element_type=jnp.float32)
            * score_scale
        )
        .astype(jnp.bfloat16)
        .reshape(row_count, -1)
    )
    gathered_query, gathered_dattn = (
        lax.all_gather(queries, "seq", axis=0, tiled=True),
        lax.all_gather(d_blocks, "seq", axis=0, tiled=True),
    )
    gathered_max, gathered_total, gathered_delta = (
        lax.all_gather(row_max, "seq", axis=0, tiled=True),
        lax.all_gather(totals, "seq", axis=0, tiled=True),
        lax.all_gather(row_delta, "seq", axis=0, tiled=True),
    )
    owners = first_block + jnp.arange(local_blocks)
    live_slots = jnp.arange(MAXN)[None, :] < counts_all[:, None]
    listed = jnp.any(
        (lists_all[:, :, None] == owners[None, None, :]) & live_slots[:, :, None], axis=1
    )
    groups = slab_blocks // 8
    own_keys = split_heads(key_rows)
    own_values = split_heads(value_rows)

    def regroup(matrix):
        return matrix.reshape((groups, 8) + matrix.shape[1:])

    def accumulate(carry, group_data):
        group_query, group_dattn, group_max, group_total, group_delta, group_listed = group_data
        group_query = split_heads(group_query)
        group_dattn = split_heads(group_dattn)
        group_scores = (
            jnp.einsum(
                "cqhd,ikhd->cihqk", group_query, own_keys, preferred_element_type=jnp.float32
            )
            * score_scale
        )
        group_scores = jnp.where(group_listed[:, :, None, None, None], group_scores, -1e30)
        group_probs = (
            jnp.exp(group_scores - group_max[:, None, :, :, None])
            / group_total[:, None, :, :, None]
        )
        group_dprobs = jnp.einsum(
            "cqhd,ikhd->cihqk", group_dattn, own_values, preferred_element_type=jnp.float32
        )
        group_dscores = (group_probs * (group_dprobs - group_delta[:, None, :, :, None])).astype(
            jnp.bfloat16
        )
        key_next = carry[0] + jnp.einsum(
            "cihqk,cqhd->ikhd", group_dscores, group_query, preferred_element_type=jnp.float32
        )
        value_next = carry[1] + jnp.einsum(
            "cihqk,cqhd->ikhd",
            group_probs.astype(jnp.bfloat16),
            group_dattn,
            preferred_element_type=jnp.float32,
        )
        return ((key_next, value_next), None)

    zero_sum = jnp.zeros((local_blocks, BLOCK, HEADS, HEAD_DIM), jnp.float32)
    group_inputs = (
        regroup(gathered_query),
        regroup(gathered_dattn),
        regroup(gathered_max),
        regroup(gathered_total),
        regroup(gathered_delta),
        regroup(listed),
    )
    (key_heads, value_heads), _ = lax.scan(accumulate, (zero_sum, zero_sum), group_inputs)
    key_sum = (key_heads * score_scale).reshape(local_blocks, BLOCK, -1)
    value_sum = value_heads.reshape(local_blocks, BLOCK, -1)
    d_keys = key_sum.astype(jnp.bfloat16).reshape(row_count, -1)
    d_values = value_sum.astype(jnp.bfloat16).reshape(row_count, -1)
    stacked = jnp.concatenate([d_queries, d_keys, d_values], axis=1)
    w_joined = jnp.concatenate([w_query, w_key, w_value], axis=1)
    d_inputs = lax.dot_general(
        stacked, w_joined, (((1,), (1,)), ((), ())), preferred_element_type=jnp.float32
    ).astype(jnp.bfloat16)
    grad_joined = lax.dot_general(
        inputs, stacked, (((0,), (0,)), ((), ())), preferred_element_type=jnp.float32
    )
    width_model = inputs.shape[1]
    grad_three = jnp.transpose(grad_joined.reshape(width_model, 3, -1), (1, 0, 2))
    grads = jnp.concatenate([grad_three, grad_out[None]], axis=0)
    within_slab = lax.psum_scatter(
        grads.astype(jnp.bfloat16), "seq", scatter_dimension=1, tiled=True
    )
    summed = lax.psum_scatter(within_slab, "rep", scatter_dimension=1, tiled=True).astype(
        jnp.float32
    )
    return (output[None], d_inputs[None], summed)


def solution(mesh):
    placed = (
        P("rep", "seq", None),
        P("rep", "seq", None),
        P(),
        P("rep", None, None),
        P("rep", None),
    )
    n, reps = mesh.shape["seq"], mesh.shape["rep"]
    run = functools.partial(by_heads, n, reps) if n == HEADS else body
    return jax.shard_map(
        run,
        mesh=mesh,
        in_specs=placed,
        out_specs=(P("rep", "seq", None), P("rep", "seq", None), P(None, ("seq", "rep"), None)),
        check_vma=False,
    )
```

profile of v0, /device:TPU:1, one launch (start us, length us, event | category | flops | bytes accessed | tf_op | source)
XLA Modules:
  0.0 51.8 jit_solution(9557821021702864301)
XLA Ops:
  0.6 0.0 copy-start
  0.6 0.7 %copy-done = s32[1,8,27]{2,1,0:T(8,128)S(1)} copy-done((s32[1,8,27]{2,1,0:T(8,128)S(1)}, s32[1,8,27]{2,1,0:T(8,128)}, u32[]{:S(2)}) %copy-start) | copy-done | bytes 888
  1.3 0.0 copy-start.1
  1.3 0.7 %copy-done.1 = s32[1,8]{1,0:T(1,128)S(1)} copy-done((s32[1,8]{1,0:T(1,128)S(1)}, s32[1,8]{1,0:T(1,128)}, u32[]{:S(2)}) %copy-start.1) | copy-done | bytes 56
  2.0 47.7 %shard_map.76 = (bf16[1,128,1024]{2,1,0:T(8,128)(2,1)S(1)}, bf16[1,128,1024]{2,1,0:T(8,128)(2,1)S(1)}, f32[4,32,512]{2,1,0:T(8,128)S(1)}) custom-call(bf16[1,128,1024]{2,1,0:T(8,128)(2,1)} %tok_hbm.1, bf16[1,128,1024]{2,1,0:T(8,128)(2,1)} %cot_hbm.1, bf16[4,1024,512]{2,1,0:T(8,128)(2,1)} %w_hbm.1, s32[1,8,27]{2,1,0:T(8,128)S(1)} %copy-done, s32[1,8]{1,0:T(1,128)S(1)} %copy-done.1), custom_call_target="tpu_custom_call" | custom-call | flops 3000000000 | bytes 6291456 | tf_op jit(solution)/shard_map/pallas_call | solution.py:390
  49.7 0.7 %copy.11 = bf16[1,128,1024]{2,1,0:T(8,128)(2,1)} copy(bf16[1,128,1024]{2,1,0:T(8,128)(2,1)S(1)} %get-tuple-element.6) | data formatting | bytes 524288
  50.4 0.7 %copy.12 = bf16[1,128,1024]{2,1,0:T(8,128)(2,1)} copy(bf16[1,128,1024]{2,1,0:T(8,128)(2,1)S(1)} %get-tuple-element.7) | data formatting | bytes 524288
  51.1 0.7 %copy.13 = f32[4,32,512]{2,1,0:T(8,128)} copy(f32[4,32,512]{2,1,0:T(8,128)S(1)} %get-tuple-element.8) | data formatting | bytes 524288
Async XLA Ops:
  0.6 0.7 %copy-start = (s32[1,8,27]{2,1,0:T(8,128)S(1)}, s32[1,8,27]{2,1,0:T(8,128)}, u32[]{:S(2)}) copy-start(s32[1,8,27]{2,1,0:T(8,128)} %lists.1) | copy-start | bytes 2596
  1.3 0.7 %copy-start.1 = (s32[1,8]{1,0:T(1,128)S(1)}, s32[1,8]{1,0:T(1,128)}, u32[]{:S(2)}) copy-start(s32[1,8]{1,0:T(1,128)} %counts.1) | copy-start | bytes 100
where the time goes:
time: 52 us; the launch traced here: 51.8 us
  Pallas kernels  47.7 us (92%)
  local copies, waits for them, and re-layouts  3.44 us (7%)
  between operations  0.65 us (1%)
    pallas_call x1, Pallas kernels, by_heads(): pl.pallas_call(functools.partial(layer_kernel, n, reps), out_shape=(jax.S...  47.7 us
    unnamed x7, local copies, waits for them, and re-layouts  3.44 us

commit v1 on v0

--- a/solution.py
+++ b/solution.py
@@ -268,6 +268,7 @@
     for b in range(n):
         rows = slice(b * BLOCK, (b + 1) * BLOCK)
         bk[0, rows] = jnp.concatenate([att_all[rows], dvt[:, rows].T.astype(BF16)], axis=1)
+    forward_cols(1)
     each_peer(lambda to: back_out(to, 0).start())
 
     def backward(i, carry):
@@ -321,7 +322,6 @@
 
     low, high = slice(0, hd), slice(hd, 2 * hd)
     lax.fori_loop(0, 2, backward, 0, unroll=2)
-    forward_cols(1)
     finish_cols(0)
     pair_in(0).wait_recv()
     product((2,), 0, 0, (high,))

time: 52 us -> 52 us (level)
  no operation moved by 1% of the time
where the time goes in v1:
time: 52 us; the launch traced here: 51.8 us
  Pallas kernels  47.7 us (92%)
  local copies, waits for them, and re-layouts  3.44 us (7%)
  between operations  0.65 us (1%)
    pallas_call x1, Pallas kernels, by_heads(): pl.pallas_call(functools.partial(layer_kernel, n, reps), out_shape=(jax.S...  47.7 us
    unnamed x7, local copies, waits for them, and re-layouts  3.44 us

profile of v1, /device:TPU:1, one launch (start us, length us, event | category | flops | bytes accessed | tf_op | source)
XLA Modules:
  0.0 51.8 jit_solution(17523807969845779450)
XLA Ops:
  0.6 0.0 copy-start
  0.6 0.7 %copy-done = s32[1,8,27]{2,1,0:T(8,128)S(1)} copy-done((s32[1,8,27]{2,1,0:T(8,128)S(1)}, s32[1,8,27]{2,1,0:T(8,128)}, u32[]{:S(2)}) %copy-start) | copy-done | bytes 888
  1.3 0.0 copy-start.1
  1.3 0.7 %copy-done.1 = s32[1,8]{1,0:T(1,128)S(1)} copy-done((s32[1,8]{1,0:T(1,128)S(1)}, s32[1,8]{1,0:T(1,128)}, u32[]{:S(2)}) %copy-start.1) | copy-done | bytes 56
  2.0 47.7 %shard_map.76 = (bf16[1,128,1024]{2,1,0:T(8,128)(2,1)S(1)}, bf16[1,128,1024]{2,1,0:T(8,128)(2,1)S(1)}, f32[4,32,512]{2,1,0:T(8,128)S(1)}) custom-call(bf16[1,128,1024]{2,1,0:T(8,128)(2,1)} %tok_hbm.1, bf16[1,128,1024]{2,1,0:T(8,128)(2,1)} %cot_hbm.1, bf16[4,1024,512]{2,1,0:T(8,128)(2,1)} %w_hbm.1, s32[1,8,27]{2,1,0:T(8,128)S(1)} %copy-done, s32[1,8]{1,0:T(1,128)S(1)} %copy-done.1), custom_call_target="tpu_custom_call" | custom-call | flops 3000000000 | bytes 6291456 | tf_op jit(solution)/shard_map/pallas_call | solution.py:390
  49.7 0.7 %copy.11 = bf16[1,128,1024]{2,1,0:T(8,128)(2,1)} copy(bf16[1,128,1024]{2,1,0:T(8,128)(2,1)S(1)} %get-tuple-element.6) | data formatting | bytes 524288
  50.4 0.7 %copy.12 = bf16[1,128,1024]{2,1,0:T(8,128)(2,1)} copy(bf16[1,128,1024]{2,1,0:T(8,128)(2,1)S(1)} %get-tuple-element.7) | data formatting | bytes 524288
  51.1 0.7 %copy.13 = f32[4,32,512]{2,1,0:T(8,128)} copy(f32[4,32,512]{2,1,0:T(8,128)S(1)} %get-tuple-element.8) | data formatting | bytes 524288
Async XLA Ops:
  0.6 0.7 %copy-start = (s32[1,8,27]{2,1,0:T(8,128)S(1)}, s32[1,8,27]{2,1,0:T(8,128)}, u32[]{:S(2)}) copy-start(s32[1,8,27]{2,1,0:T(8,128)} %lists.1) | copy-start | bytes 2596
  1.3 0.7 %copy-start.1 = (s32[1,8]{1,0:T(1,128)S(1)}, s32[1,8]{1,0:T(1,128)}, u32[]{:S(2)}) copy-start(s32[1,8]{1,0:T(1,128)} %counts.1) | copy-start | bytes 100
